TPU v7x, 32 devices: a whole 2x2x4 slice. The times are simulated.
32 devices in a mesh: groups: 2 (over x), dp: 4 (over y, core), hidden: 4 (over z).
Axes of the slice: x: 2, y: 2, z: 4, core: 2. Of those that a mesh axis runs over, the one named last changes fastest.
Arguments:
- activations: bfloat16 [24576, 8192], P(('groups', 'dp'), 'hidden'), parts along dimension 0, may hold values from -6 to 6
- cotangent: bfloat16 [24576, 8192], P(('groups', 'dp'), 'hidden'), parts along dimension 0
- up_factor_matrix: bfloat16 [8192, 64], P('hidden'), may hold values from -0.0625 to 0.0625
- input_sketch: bfloat16 [8192, 128], P('hidden'), may hold values from -0.0625 to 0.0625
- rank_sketch: float32 [64, 32], replicated, may hold values from -0.75 to 0.75
Outputs:
- features: bfloat16 [48, 4096], P(('groups', 'dp'), 'hidden'), parts along dimension 0
- scores: float32 [48, 24], P(('groups', 'dp'), 'hidden'), parts along dimension 0
There are 2 independent parts, one for each index of `groups`. A program takes and returns all parts, laid end to end along the dimension named above; an argument that names none is the same for every part. Nothing has to cross between parts.
All inputs are finite; a program needn't handle non-finite values.
Results may differ from a plain program's by a relative error of at most 0.0017.
Values may be sent and summed in bfloat16 or wider, within the bound.
A program may use at most 64 MiB of HBM per device.

v0:
```python
import math

import jax
import jax.numpy as jnp
from jax import lax
from jax.sharding import PartitionSpec as P

FEAT = 4096
SEQ = 512


epsilon = 1e-05


def outer_product_sums(rank_rows, input_rows, examples):
    rank_rows = rank_rows.reshape(examples, SEQ, rank_rows.shape[1])
    input_rows = input_rows.reshape(examples, SEQ, input_rows.shape[1])
    return jnp.einsum("esa,esb->eab", rank_rows, input_rows, precision=lax.Precision.HIGHEST)


def per_device(activations, cotangent, up_factor_matrix, input_sketch, rank_sketch):
    shards = lax.axis_size("hidden")
    own_cols = rank_sketch.shape[1] // shards
    examples = activations.shape[0] // SEQ
    backward_pass = jnp.dot(cotangent, up_factor_matrix, preferred_element_type=jnp.float32)
    rank_part = jnp.dot(backward_pass, rank_sketch, precision=lax.Precision.HIGHEST)
    input_part = jnp.dot(activations, input_sketch, preferred_element_type=jnp.float32)
    rank_full, input_full = lax.psum((rank_part, input_part), "hidden")
    rank_own = lax.dynamic_slice_in_dim(rank_full, lax.axis_index("hidden") * own_cols, own_cols, 1)
    feat_block = outer_product_sums(rank_own, input_full, examples)
    features = feat_block.reshape(examples, -1).astype(jnp.bfloat16)
    widened = features.astype(jnp.float32)
    all_count = examples * lax.axis_size("dp")
    squares = lax.psum(jnp.sum(widened * widened, axis=0), "dp")
    weighted = widened * (1.0 / (squares / all_count + epsilon))
    partial_scores = jnp.dot(
        weighted,
        lax.all_gather(features, "dp", axis=0, tiled=True).astype(jnp.float32).T,
        precision=lax.Precision.HIGHEST,
    )
    scores = lax.psum_scatter(
        partial_scores / math.sqrt(FEAT), "hidden", scatter_dimension=1, tiled=True
    )
    return (features, scores)


def solution(mesh):
    placed = (
        P(("groups", "dp"), "hidden"),
        P(("groups", "dp"), "hidden"),
        P("hidden", None),
        P("hidden", None),
        P(),
    )
    return jax.shard_map(
        per_device,
        mesh=mesh,
        in_specs=placed,
        out_specs=(P(("groups", "dp"), "hidden"), P(("groups", "dp"), "hidden")),
        check_vma=False,
    )
```

profile of v0, /device:TPU:0, one launch (start us, length us, event | category | flops | bytes accessed | tf_op | source)
XLA Modules:
  0.0 139.9 jit_solution(18415344260464060510)
XLA Ops:
  7.2 0.0 copy-start
  7.2 0.0 copy-start.2
  7.2 0.0 all-reduce.4.cloned.1.call-start
  7.2 0.0 copy-start.3
  7.2 8.6 %fusion.3 = f32[3072,64]{0,1:T(8,128)S(1)} fusion(bf16[3072,2048]{1,0:T(8,128)(2,1)} %param.6, bf16[2048,64]{0,1:T(8,128)(2,1)} %param.7), kind=kOutput, calls=%fused_computation.10 | convolution fusion | flops 805306368 | bytes 13631488 | tf_op jit(solution)/shard_map/dot_general | solution.py:25
  15.9 0.0 copy-done.2
  15.9 0.0 copy-start.4
  15.9 1.3 fusion.4
  17.2 0.0 copy-done
  17.2 0.0 copy-done.3
  17.2 4.6 %fusion.5 = f32[3072,128]{1,0:T(8,128)} fusion(bf16[3072,2048]{1,0:T(8,128)(2,1)S(1)} %copy-done.3, bf16[2048,128]{1,0:T(8,128)(2,1)S(1)} %copy-done), kind=kOutput, calls=%fused_computation.12 | convolution fusion | flops 1610612736 | bytes 14680064 | tf_op jit(solution)/shard_map/dot_general | solution.py:27
  21.8 0.0 all-reduce.4.cloned.1.call-update
  21.8 0.0 copy-done.4
  21.8 0.6 dynamic-slice
  23.1 83.8 %all-reduce.4.cloned.1.call-done = (f32[3072,32]{0,1:T(8,128)}, f32[6,512,128]{2,1,0:T(8,128)}) async-done(((f32[3072,32]{0,1:T(8,128)}, f32[6,512,128]{2,1,0:T(8,128)}), (f32[3072,32]{0,1:T(8,128)}, f32[6,512,128]{2,1,0:T(8,128)})) %all-reduce.4.cloned.1.call-update) | async-done | bytes 1966096 | tf_op jit(solution)/shard_map/psum | solution.py:28
  106.9 0.9 constant_dynamic-slice_fusion.1
  107.8 2.3 %multiply_reduce_fusion = (f32[8,128]{1,0:T(8,128)S(1)}, bf16[6,8,128]{2,1,0:T(8,128)(2,1)S(1)}) fusion(f32[6,512,8]{1,2,0:T(8,128)S(1)} %bitcast.20, f32[6,512,128]{2,1,0:T(8,128)} %get-tuple-element.3), kind=kOutput, calls=%fused_computation.4 | convolution fusion | flops 37772288 | bytes 1687552 | tf_op jit(solution)/shard_map/esa,esb->eab/dot_general | solution.py:18
  110.2 0.0 copy-start.1
  110.2 5.2 %all-gather = bf16[4,6,1024]{2,1,0:T(8,128)(2,1)S(1)} all-gather(bf16[1,6,1024]{2,1,0:T(8,128)(2,1)S(1)} %reshape.16), channel_id=1, replica_groups=mesh['groups'=2,'dp'=4,'hidden'=4] {'dp'}, dimensions={0}, use_global_device_ids=true | all-gather | bytes 61440 | tf_op jit(solution)/shard_map/all_gather | solution.py:38
  115.4 7.1 %psum.23 = f32[1024]{0:T(1024)S(1)} all-reduce(f32[1024]{0:T(1024)S(1)} %bitcast.24), channel_id=1, replica_groups=mesh['groups'=2,'dp'=4,'hidden'=4] {'dp'}, use_global_device_ids=true, to_apply=%region_3.0 | all-reduce | flops 1024 | bytes 8192 | tf_op jit(solution)/shard_map/psum | solution.py:34
  122.5 0.1 convolution_multiply_fusion
  122.7 9.8 %all-reduce = f32[6,24]{1,0:T(8,128)S(1)} all-reduce(f32[6,24]{1,0:T(8,128)S(1)} %convolution_multiply_fusion), channel_id=2, replica_groups=mesh['groups'=2,'dp'=4,'hidden'=4] {'hidden'}, use_global_device_ids=true, to_apply=%region_4.0.clone | all-reduce | flops 144 | bytes 1152
  132.4 0.7 constant_dynamic-slice_fusion
  133.1 0.0 copy-done.1
  (4 shorter events, 0.1 us)
Async XLA Ops:
  7.2 10.0 %copy-start = (bf16[2048,128]{1,0:T(8,128)(2,1)S(1)}, bf16[2048,128]{1,0:T(8,128)(2,1)}, u32[]{:S(2)}) copy-start(bf16[2048,128]{1,0:T(8,128)(2,1)} %param.8) | copy-start | bytes 1572868
  7.2 8.7 %copy-start.2 = (f32[64,32]{0,1:T(8,128)S(1)}, f32[64,32]{0,1:T(8,128)}, u32[]{:S(2)}) copy-start(f32[64,32]{0,1:T(8,128)} %param.9) | copy-start | bytes 24580
  7.2 99.7 %all-reduce.4.cloned.1.call-start = ((), (), s32[]{:S(2)}) async-start(), calls=%async_computation | async-start | bytes 3932160 | tf_op jit(solution)/shard_map/psum | solution.py:28
  7.2 10.0 %copy-start.3 = (bf16[3072,2048]{1,0:T(8,128)(2,1)S(1)}, bf16[3072,2048]{1,0:T(8,128)(2,1)}, u32[]{:S(2)}) copy-start(bf16[3072,2048]{1,0:T(8,128)(2,1)} %param.5) | copy-start | bytes 37748740
  15.9 5.9 %copy-start.4 = (u32[32]{0:T(128)S(1)}, u32[32]{0:T(128)}, u32[]{:S(2)}) copy-start(u32[32]{0:T(128)} %constant.24) | copy-start | bytes 388
  110.2 22.9 %copy-start.1 = (bf16[1,6,8,128]{3,1,2,0:T(8,128)(2,1)}, bf16[1,6,8,128]{3,1,2,0:T(8,128)(2,1)S(1)}, u32[]{:S(2)}) copy-start(bf16[1,6,8,128]{3,1,2,0:T(8,128)(2,1)S(1)} %copy.11) | copy-start | bytes 36868
Sparse Core Ops, SparseCore 0:
  21.9 84.9 all-reduce.3
where the time goes:
time: 140 us
  waiting for transfers between devices  83.9 us (60%)
  blocking collectives  22.1 us (16%)
  matrix products  16.9 us (12%)
  between operations  14.8 us (11%)
  local copies, waits for them, and re-layouts  2.26 us (2%)
    psum x1, waiting for transfers between devices, per_device(): rank_full, input_full = lax.psum((rank_part, input_part), 'hidden')  83.8 us
    unnamed x1, blocking collectives  9.77 us
    dot_general x1, matrix products, per_device(): jnp.dot(cotangent, up_factor_matrix, preferred_element_type=jnp.float32)  8.64 us
    psum x1, blocking collectives, per_device(): squares = lax.psum(jnp.sum(widened * widened, axis=0), 'dp')  7.08 us
    all_gather x1, blocking collectives, per_device(): lax.all_gather(features, 'dp', axis=0, tiled=True).astype(jnp.float32)  5.25 us
    dot_general x1, matrix products, per_device(): jnp.dot(activations, input_sketch, preferred_element_type=jnp.float32)  4.58 us
  transfers between devices with their start and end apart: 1, of which 1 were waited for; matrix products, arithmetic and copies ran while one was open for 0% of the time, Pallas kernels for 0%

commit v1 on v0

v1 whole, which is shorter than its diff:
```python
import functools
import math

import jax
import jax.numpy as jnp
from jax import lax
from jax.experimental import pallas as pl
from jax.experimental.pallas import tpu as pltpu
from jax.sharding import PartitionSpec as P

SEQ = 512
PARTS = 2
AHEAD = 4
GROUP = 2
epsilon = 1e-05
MESH = pl.DeviceIdType.MESH
F32, BF16 = jnp.float32, jnp.bfloat16


def halves(x):
    hi = x.astype(BF16)
    return hi, (x - hi.astype(F32)).astype(BF16)


def kernel(
    n, m, act, cot, upf, sketch, rank, feat_out, score_out,
    cotv, actv, upv, skv, rkv, brv, inp, own, pin, sin, pout, sout,
    fpart, fin, rounded, mine, theirs, everyone, part, parts_in,
    load_sem, p_send, p_recv, s_send, s_recv,
    f_send, f_recv, g_send, g_recv, c_send, c_recv,
):
    h, d = lax.axis_index("hidden"), lax.axis_index("dp")
    count = cotv.shape[0]
    k_r, k_in = rkv.shape[1], skv.shape[1]
    rows = k_r // n
    width = SEQ // PARTS

    barrier = pltpu.get_barrier_semaphore()
    for k in range(1, n):
        pl.semaphore_signal(
            barrier, inc=1, device_id={"hidden": lax.rem(h + k, n)}, device_id_type=MESH)
    for k in range(1, m):
        pl.semaphore_signal(
            barrier, inc=1, device_id={"dp": lax.rem(d + k, m)}, device_id_type=MESH)

    def load(s):
        c = s % count
        big, held = (cot, cotv) if s < count else (act, actv)
        return pltpu.make_async_copy(big.at[pl.ds(c * SEQ, SEQ)], held.at[c], load_sem.at[s])

    load_up = pltpu.make_async_copy(upf, upv, load_sem.at[2 * count])
    load_rank = pltpu.make_async_copy(rank, rkv, load_sem.at[2 * count + 1])
    load_sketch = pltpu.make_async_copy(sketch, skv, load_sem.at[2 * count + 2])
    load_up.start()
    load_rank.start()
    for s in range(AHEAD):
        load(s).start()
    load_sketch.start()

    @pl.when(h == 0)
    def _():
        pin[...] = jnp.zeros_like(pin)

    @pl.when(h == n - 1)
    def _():
        sin[...] = jnp.zeros_like(sin)

    load_rank.wait()
    load_up.wait()
    r1 = rkv[...].astype(BF16)
    rest = rkv[...] - r1.astype(F32)
    r2 = rest.astype(BF16)
    r3 = (rest - r2.astype(F32)).astype(BF16)
    wide = jnp.dot(upv[...], jnp.concatenate([r1, r2, r3], 1), preferred_element_type=F32)
    merged = wide[:, :k_r] + (wide[:, k_r:2 * k_r] + wide[:, 2 * k_r:])
    hi, lo = halves(merged)
    brv[...] = jnp.concatenate([hi, lo], 1)

    def to_right(q, source):
        return pltpu.make_async_remote_copy(
            source.at[q], pin.at[q], p_send.at[q], p_recv.at[q],
            device_id={"hidden": lax.rem(h + 1, n)}, device_id_type=MESH)

    def to_left(q, source):
        return pltpu.make_async_remote_copy(
            source.at[q], sin.at[q], s_send.at[q], s_recv.at[q],
            device_id={"hidden": lax.rem(h + n - 1, n)}, device_id_type=MESH)

    def f_copy(k, g):
        return pltpu.make_async_remote_copy(
            fpart.at[g, lax.rem(h + k, n)], fin.at[k - 1, g],
            f_send.at[k - 1, g], f_recv.at[k - 1, g],
            device_id={"hidden": lax.rem(h + k, n)}, device_id_type=MESH)

    def product(s):
        load(s).wait()
        if s + AHEAD < 2 * count:
            load(s + AHEAD).start()
        c = s % count
        if s < count:
            flat = jnp.dot(cotv[c], brv[...], preferred_element_type=F32).T
            total = flat[:k_r] + flat[k_r:]
            for j in range(PARTS):
                own[c * PARTS + j] = total[:, j * width:(j + 1) * width]
            if s == 0:
                pl.semaphore_wait(barrier, n + m - 2)

            @pl.when(h == 0)
            def _():
                for j in range(PARTS):
                    to_right(c * PARTS + j, own).start()

            @pl.when(h == n - 1)
            def _():
                for j in range(PARTS):
                    to_left(c * PARTS + j, own).start()
        else:
            if s == count:
                load_sketch.wait()
            side = jnp.dot(actv[c], skv[...], preferred_element_type=F32)
            hi, lo = halves(side)
            inp[c] = jnp.concatenate([hi, lo], 1)

    def forward(q, place, right):
        @pl.when(h == place)
        def _():
            if right:
                to_right(q, pout).wait_recv()
                pout[q] = pin[q] + own[q]
                to_right(q, pout).start()
            else:
                to_left(q, sout).wait_recv()
                sout[q] = sin[q] + own[q]
                to_left(q, sout).start()

    def finish(c):
        span = range(c * PARTS, (c + 1) * PARTS)

        @pl.when(h == n - 1)
        def _():
            for q in span:
                to_right(q, pout).wait_recv()

        @pl.when(h == 0)
        def _():
            for q in span:
                to_left(q, sout).wait_recv()

        total = jnp.concatenate([own[q] + (pin[q] + sin[q]) for q in span], 1)
        hi, lo = halves(total)
        out = jnp.dot(jnp.concatenate([hi, lo], 0), inp[c], preferred_element_type=F32)
        block = out[:k_r, :k_in] + (
            (out[:k_r, k_in:] + out[k_r:, :k_in]) + out[k_r:, k_in:])
        g, j = c // GROUP, c % GROUP
        for k in range(n):
            fpart[g, k, j] = block[k * rows:(k + 1) * rows]
        if j == GROUP - 1:
            for k in range(1, n):
                f_copy(k, g).start()

    events = []
    for s in range(2 * count):
        events.append((float(s), 0, functools.partial(product, s)))
    step_link, step_hop = 2.3 / PARTS, 1.5
    for q in range(count * PARTS):
        ready = 1 + q // PARTS

        def arrival(hops):
            first = 1 + hops * (step_link + step_hop) + step_link * q
            return max(first, ready + hops * (step_link + step_hop))

        for place in range(1, n - 1):
            events.append((arrival(place), 1, functools.partial(forward, q, place, True)))
            events.append((arrival(n - 1 - place), 1, functools.partial(forward, q, place, False)))
        if q % PARTS == PARTS - 1:
            c = q // PARTS
            events.append((max(arrival(n - 1), count + c + 1), 2, functools.partial(finish, c)))
    for event in sorted(events, key=lambda e: e[:2]):
        event[2]()

    groups = count // GROUP
    for g in range(groups):
        for k in range(1, n):
            f_copy(k, g).wait_recv()
        for j in range(GROUP):
            value = fpart[g, h, j]
            for k in range(1, n):
                value = value + fin[k - 1, g, j]
            rounded[pl.ds((g * GROUP + j) * rows, rows), :] = value.astype(BF16).astype(F32)

    used = count * rows
    mine[pl.ds(0, used), :] = rounded[...].astype(BF16)

    def g_copy(k):
        return pltpu.make_async_remote_copy(
            mine, theirs.at[k - 1], g_send.at[k - 1], g_recv.at[k - 1],
            device_id={"dp": lax.rem(d + k, m)}, device_id_type=MESH)

    for k in range(1, m):
        g_copy(k).start()
    everyone[pl.ds(pl.multiple_of(d * used, 8), used), :] = rounded[...]
    for a in range(rows):
        feat_out[:, a * k_in:(a + 1) * k_in] = (
            rounded[pl.ds(a, count, stride=rows), :].astype(BF16))
    part[...] = jnp.zeros_like(part)
    for k in range(1, m):
        g_copy(k).wait_recv()
        sender = lax.rem(d + m - k, m)
        everyone[pl.ds(pl.multiple_of(sender * used, 8), used), :] = (
            theirs[k - 1][:used].astype(F32))

    columns, scaled = [], []
    for a in range(rows):
        y = everyone[pl.ds(a, m * count, stride=rows), :]
        squares = jnp.sum(y * y, axis=0, keepdims=True)
        weight = 1.0 / (squares / (m * count) + epsilon)
        columns.append(y.astype(BF16))
        scaled.append(rounded[pl.ds(a, count, stride=rows), :] * weight)
    y = jnp.concatenate(columns, 1)
    hi, lo = halves(jnp.concatenate(scaled, 1))
    across = (((1,), (1,)), ((), ()))
    dots = lax.dot_general(hi, y, across, preferred_element_type=F32) + lax.dot_general(
        lo, y, across, preferred_element_type=F32)
    part[pl.ds(0, count), pl.ds(0, m * count)] = dots / math.sqrt(k_r * k_in)

    def c_copy(k):
        return pltpu.make_async_remote_copy(
            part, parts_in.at[k - 1], c_send.at[k - 1], c_recv.at[k - 1],
            device_id={"hidden": lax.rem(h + k, n)}, device_id_type=MESH)

    for k in range(1, n):
        c_copy(k).start()
    total = part[...]
    for k in range(1, n):
        c_copy(k).wait_recv()
        total = total + parts_in[k - 1]
    cols = score_out.shape[1]
    for place in range(n):
        @pl.when(h == place)
        def _():
            score_out[...] = total[:count, place * cols:(place + 1) * cols]

    @pl.when(h < n - 1)
    def _():
        for q in range(count * PARTS):
            to_right(q, own).wait_send()

    @pl.when(h > 0)
    def _():
        for q in range(count * PARTS):
            to_left(q, own).wait_send()

    for k in range(1, n):
        for g in range(groups):
            f_copy(k, g).wait_send()
        c_copy(k).wait_send()
    for k in range(1, m):
        g_copy(k).wait_send()


def per_device(n, m, activations, cotangent, up_factor_matrix, input_sketch, rank_sketch):
    tokens, depth = activations.shape
    count = tokens // SEQ
    low, k_r = rank_sketch.shape
    k_in = input_sketch.shape[1]
    rows = k_r // n
    used = count * rows
    padded = -(-used // 16) * 16
    lanes = -(-m * count // 128) * 128
    pieces, width = count * PARTS, SEQ // PARTS
    groups = count // GROUP
    vm, dma = pltpu.VMEM, pltpu.SemaphoreType.DMA
    piece = vm((pieces, k_r, width), F32)
    return pl.pallas_call(
        functools.partial(kernel, n, m),
        out_shape=(
            jax.ShapeDtypeStruct((count, rows * k_in), BF16),
            jax.ShapeDtypeStruct((count, m * count // n), F32),
        ),
        in_specs=[pl.BlockSpec(memory_space=pl.ANY)] * 5,
        out_specs=(pl.BlockSpec(memory_space=pltpu.VMEM),) * 2,
        scratch_shapes=[
            vm((count, SEQ, depth), BF16),
            vm((count, SEQ, depth), BF16),
            vm((depth, low), BF16),
            vm((depth, k_in), BF16),
            vm((low, k_r), F32),
            vm((depth, 2 * k_r), BF16),
            vm((count, SEQ, 2 * k_in), BF16),
            piece, piece, piece, piece, piece,
            vm((groups, n, GROUP, rows, k_in), F32),
            vm((n - 1, groups, GROUP, rows, k_in), F32),
            vm((used, k_in), F32),
            vm((padded, k_in), BF16),
            vm((m - 1, padded, k_in), BF16),
            vm((m * used, k_in), F32),
            vm((8, lanes), F32),
            vm((n - 1, 8, lanes), F32),
            dma((2 * count + 3,)),
            dma((pieces,)), dma((pieces,)), dma((pieces,)), dma((pieces,)),
            dma((n - 1, groups)), dma((n - 1, groups)),
            dma((m - 1,)), dma((m - 1,)),
            dma((n - 1,)), dma((n - 1,)),
        ],
        compiler_params=pltpu.CompilerParams(
            collective_id=0, has_side_effects=True, vmem_limit_bytes=52 * 2**20),
        cost_estimate=pl.CostEstimate(
            flops=2 * tokens * depth * (2 * k_r + k_in),
            bytes_accessed=4 * tokens * depth, transcendentals=0),
    )(activations, cotangent, up_factor_matrix, input_sketch, rank_sketch)


def solution(mesh):
    placed = (
        P(("groups", "dp"), "hidden"),
        P(("groups", "dp"), "hidden"),
        P("hidden", None),
        P("hidden", None),
        P(),
    )
    return jax.shard_map(
        functools.partial(per_device, mesh.shape["hidden"], mesh.shape["dp"]),
        mesh=mesh,
        in_specs=placed,
        out_specs=(P(("groups", "dp"), "hidden"), P(("groups", "dp"), "hidden")),
        check_vma=False,
    )
```

time: 140 us -> 46.4 us (0.33)
  waiting for transfers between devices: 83.9 us -> 0 us
  Pallas kernels: 0 us -> 41.2 us
  blocking collectives: 22.1 us -> 0 us
  matrix products: 16.9 us -> 0 us
  between operations: 14.8 us -> 0.65 us
  local copies, waits for them, and re-layouts: 2.26 us -> 4.26 us
    psum x1 -> x0, waiting for transfers between devices: 83.8 us -> none  [per_device(): rank_full, input_full = lax.psum((rank_part, input_part), 'hidden')]
    pallas_call x0 -> x1, Pallas kernels: none -> 41.2 us  [per_device(): pl.pallas_call(functools.partial(kernel, n, m), out_shape=(jax.ShapeDtype...]
    dot_general x5 -> x0, matrix products: 16.9 us -> none  [the longest x1 8.64 us: per_device(): jnp.dot(cotangent, up_factor_matrix, preferred_element_type=jnp.float32)]
    unnamed x1 -> x0, blocking collectives: 9.77 us -> none
    psum x1 -> x0, blocking collectives: 7.08 us -> none  [per_device(): squares = lax.psum(jnp.sum(widened * widened, axis=0), 'dp')]
    all_gather x1 -> x0, blocking collectives: 5.25 us -> none  [per_device(): lax.all_gather(features, 'dp', axis=0, tiled=True).astype(jnp.float32)]
    unnamed x15 -> x6, local copies, waits for them, and re-layouts: 1.36 us -> 4.26 us
  transfers between devices with their start and end apart: 1 -> 0, of which waited for: 1 -> 0; matrix products, arithmetic and copies ran while one was open for 0% -> 0% of each run, Pallas kernels for 0% -> 0%
where the time goes in v1:
time: 46.4 us; the launch traced here: 46.1 us
  Pallas kernels  41.2 us (89%)
  local copies, waits for them, and re-layouts  4.26 us (9%)
  between operations  0.65 us (1%)
    pallas_call x1, Pallas kernels, per_device(): pl.pallas_call(functools.partial(kernel, n, m), out_shape=(jax.ShapeDtype...  41.2 us
    unnamed x6, local copies, waits for them, and re-layouts  4.26 us

profile of v1, /device:TPU:0, one launch (start us, length us, event | category | flops | bytes accessed | tf_op | source)
XLA Modules:
  0.0 46.1 jit_solution(6480470216165317083)
XLA Ops:
  0.6 0.8 %copy.8.rank = f32[64,32]{1,0:T(8,128)S(1)} copy(f32[64,32]{0,1:T(8,128)} %param.9) | data formatting | bytes 16384 | tf_op args[4]
  1.4 1.2 %copy.7.upf = bf16[2048,64]{1,0:T(8,128)(2,1)S(1)} copy(bf16[2048,64]{0,1:T(8,128)(2,1)} %param.7) | data formatting | bytes 524288 | tf_op args[2]
  2.7 0.0 copy-start
  2.7 1.0 %copy-done = bf16[2048,128]{1,0:T(8,128)(2,1)S(1)} copy-done((bf16[2048,128]{1,0:T(8,128)(2,1)S(1)}, bf16[2048,128]{1,0:T(8,128)(2,1)}, u32[]{:S(2)}) %copy-start) | copy-done | bytes 524312
  3.7 41.2 %shard_map.68 = (bf16[6,1024]{1,0:T(8,128)(2,1)S(1)}, f32[6,6]{1,0:T(8,128)S(1)}) custom-call(bf16[3072,2048]{1,0:T(8,128)(2,1)} %act.1, bf16[3072,2048]{1,0:T(8,128)(2,1)} %cot.1, bf16[2048,64]{1,0:T(8,128)(2,1)S(1)} %copy.7.upf, bf16[2048,128]{1,0:T(8,128)(2,1)S(1)} %copy-done, f32[64,32]{1,0:T(8,128)S(1)} %copy.8.rank), custom_call_target="tpu_custom_call" | custom-call | flops 2415919104 | bytes 25165824 | tf_op jit(solution)/shard_map/pallas_call | solution.py:274
  44.9 0.6 %copy.11 = bf16[6,1024]{1,0:T(8,128)(2,1)} copy(bf16[6,1024]{1,0:T(8,128)(2,1)S(1)} %get-tuple-element.4) | data formatting | bytes 24576
  45.5 0.6 %copy.12 = f32[6,6]{1,0:T(8,128)} copy(f32[6,6]{1,0:T(8,128)S(1)} %get-tuple-element.5) | data formatting | bytes 288
Async XLA Ops:
  2.7 1.0 %copy-start = (bf16[2048,128]{1,0:T(8,128)(2,1)S(1)}, bf16[2048,128]{1,0:T(8,128)(2,1)}, u32[]{:S(2)}) copy-start(bf16[2048,128]{1,0:T(8,128)(2,1)} %sketch.1) | copy-start | bytes 1572868

commit v2 on v1

v2 whole, which is shorter than its diff:
```python
import functools
import math

import jax
import jax.numpy as jnp
from jax import lax
from jax.experimental import pallas as pl
from jax.experimental.pallas import tpu as pltpu
from jax.sharding import PartitionSpec as P

SEQ = 512
PARTS = 2
AHEAD = 4
LAG = 3
epsilon = 1e-05
MESH = pl.DeviceIdType.MESH
F32, BF16 = jnp.float32, jnp.bfloat16


def halves(x):
    hi = x.astype(BF16)
    return hi, (x - hi.astype(F32)).astype(BF16)


def kernel(
    n, m, act, cot, upf, sketch, rank, feat_out, score_out,
    cotv, actv, upv, skv, rkv, brv, inp, own, pin, sin, pout, sout,
    fpart, fin, rounded, mine, theirs, everyone, part, parts_in,
    load_sem, p_send, p_recv, s_send, s_recv,
    f_send, f_recv, g_send, g_recv, c_send, c_recv,
):
    h, d = lax.axis_index("hidden"), lax.axis_index("dp")
    count = cotv.shape[0]
    k_r, k_in = rkv.shape[0], skv.shape[1]
    rows = k_r // n
    pieces, width = count * PARTS, SEQ // PARTS

    barrier = pltpu.get_barrier_semaphore()
    for k in range(1, n):
        pl.semaphore_signal(
            barrier, inc=1, device_id={"hidden": lax.rem(h + k, n)}, device_id_type=MESH)
    for k in range(1, m):
        pl.semaphore_signal(
            barrier, inc=1, device_id={"dp": lax.rem(d + k, m)}, device_id_type=MESH)

    def load(big, held, c, base):
        return pltpu.make_async_copy(
            big.at[pl.ds(pl.multiple_of(c * SEQ, SEQ), SEQ)], held.at[c], load_sem.at[base + c])

    def load_cot(c):
        return load(cot, cotv, c, 0)

    def load_act(c):
        return load(act, actv, c, count)

    load_up = pltpu.make_async_copy(upf, upv, load_sem.at[2 * count])
    load_rank = pltpu.make_async_copy(rank, rkv, load_sem.at[2 * count + 1])
    load_sketch = pltpu.make_async_copy(sketch, skv, load_sem.at[2 * count + 2])
    load_rank.start()
    load_up.start()
    for c in range(AHEAD):
        load_cot(c).start()
    load_sketch.start()

    @pl.when(h == 0)
    def _():
        pin[...] = jnp.zeros_like(pin)

    @pl.when(h == n - 1)
    def _():
        sin[...] = jnp.zeros_like(sin)

    load_rank.wait()
    load_up.wait()
    r1 = rkv[...].astype(BF16)
    rest = rkv[...] - r1.astype(F32)
    r2 = rest.astype(BF16)
    r3 = (rest - r2.astype(F32)).astype(BF16)
    wide = jnp.dot(jnp.concatenate([r1, r2, r3], 0), upv[...], preferred_element_type=F32)
    merged = wide[:k_r] + (wide[k_r:2 * k_r] + wide[2 * k_r:])
    top = merged.astype(BF16).astype(F32)
    brv[...] = jnp.concatenate([top, merged - top], 0).T.astype(BF16)

    def to_right(source, q):
        return pltpu.make_async_remote_copy(
            source.at[q], pin.at[q], p_send.at[0], p_recv.at[q],
            device_id={"hidden": lax.rem(h + 1, n)}, device_id_type=MESH)

    def to_left(source, q):
        return pltpu.make_async_remote_copy(
            source.at[q], sin.at[q], s_send.at[0], s_recv.at[q],
            device_id={"hidden": lax.rem(h + n - 1, n)}, device_id_type=MESH)

    def forward(step):
        q = step - LAG * h

        @pl.when((h > 0) & (h < n - 1) & (q >= 0) & (q < pieces))
        def _():
            to_right(pout, q).wait_recv()
            pout[q] = pin[q] + own[q]
            to_right(pout, q).start()

        p = step - LAG * (n - 1 - h)

        @pl.when((h > 0) & (h < n - 1) & (p >= 0) & (p < pieces))
        def _():
            to_left(sout, p).wait_recv()
            sout[p] = sin[p] + own[p]
            to_left(sout, p).start()

    def f_copy(k, c):
        return pltpu.make_async_remote_copy(
            fpart.at[lax.rem(h + k, n), c], fin.at[k - 1, c],
            f_send.at[k - 1], f_recv.at[k - 1],
            device_id={"hidden": lax.rem(h + k, n)}, device_id_type=MESH)

    def f_whole(k):
        return pltpu.make_async_remote_copy(
            fpart.at[lax.rem(h + k, n)], fin.at[k - 1],
            f_send.at[k - 1], f_recv.at[k - 1],
            device_id={"hidden": lax.rem(h + k, n)}, device_id_type=MESH)

    pl.semaphore_wait(barrier, n + m - 2)

    def rank_step(c, carry):
        load_cot(c).wait()

        @pl.when(c + AHEAD < count)
        def _():
            load_cot(c + AHEAD).start()

        @pl.when(c + AHEAD >= count)
        def _():
            load_act(c + AHEAD - count).start()

        flat = jnp.dot(cotv[c], brv[...], preferred_element_type=F32).T
        total = flat[:k_r] + flat[k_r:]
        for j in range(PARTS):
            own[c * PARTS + j] = total[:, j * width:(j + 1) * width]

        @pl.when(h == 0)
        def _():
            for j in range(PARTS):
                to_right(own, c * PARTS + j).start()

        @pl.when(h == n - 1)
        def _():
            for j in range(PARTS):
                to_left(own, c * PARTS + j).start()

        forward(c)
        return carry

    lax.fori_loop(0, count, rank_step, 0)
    load_sketch.wait()

    def input_step(c, carry):
        load_act(c).wait()

        @pl.when(c + AHEAD < count)
        def _():
            load_act(c + AHEAD).start()

        side = jnp.dot(actv[c], skv[...], preferred_element_type=F32)
        hi, lo = halves(side)
        inp[c] = jnp.concatenate([hi, lo], 1)
        forward(count + c)
        return carry

    lax.fori_loop(0, count, input_step, 0)

    def finish(c):
        @pl.when(h == n - 1)
        def _():
            for j in range(PARTS):
                to_right(pout, c * PARTS + j).wait_recv()

        @pl.when(h == 0)
        def _():
            for j in range(PARTS):
                to_left(sout, c * PARTS + j).wait_recv()

        total = jnp.concatenate(
            [own[q] + (pin[q] + sin[q]) for q in [c * PARTS + j for j in range(PARTS)]], 1)
        hi, lo = halves(total)
        out = jnp.dot(jnp.concatenate([hi, lo], 0), inp[c], preferred_element_type=F32)
        block = out[:k_r, :k_in] + (
            (out[:k_r, k_in:] + out[k_r:, :k_in]) + out[k_r:, k_in:])
        for k in range(n):
            fpart[k, c] = block[k * rows:(k + 1) * rows]
        for k in range(1, n):
            f_copy(k, c).start()

    late = max(0, -(-(LAG * (n - 2) + pieces - 2 * count) // PARTS) - count)

    def last_step(t, carry):
        for j in range(PARTS):
            forward(2 * count + PARTS * t + j)
        if late:
            pl.when(t >= late)(lambda: finish(t - late))
        else:
            finish(t)
        return carry

    lax.fori_loop(0, count + late, last_step, 0)

    for k in range(1, n):
        f_whole(k).wait_recv()
    for c in range(count):
        value = fpart[h, c]
        for k in range(1, n):
            value = value + fin[k - 1, c]
        rounded[pl.ds(c * rows, rows), :] = value.astype(BF16).astype(F32)

    used = count * rows
    mine[pl.ds(0, used), :] = rounded[...].astype(BF16)

    def g_copy(k):
        return pltpu.make_async_remote_copy(
            mine, theirs.at[k - 1], g_send.at[k - 1], g_recv.at[k - 1],
            device_id={"dp": lax.rem(d + k, m)}, device_id_type=MESH)

    for k in range(1, m):
        g_copy(k).start()
    everyone[pl.ds(pl.multiple_of(d * used, 8), used), :] = rounded[...]
    for a in range(rows):
        feat_out[:, a * k_in:(a + 1) * k_in] = (
            rounded[pl.ds(a, count, stride=rows), :].astype(BF16))
    part[...] = jnp.zeros_like(part)
    for k in range(1, m):
        g_copy(k).wait_recv()
        sender = lax.rem(d + m - k, m)
        everyone[pl.ds(pl.multiple_of(sender * used, 8), used), :] = (
            theirs[k - 1][:used].astype(F32))

    columns, scaled = [], []
    for a in range(rows):
        y = everyone[pl.ds(a, m * count, stride=rows), :]
        squares = jnp.sum(y * y, axis=0, keepdims=True)
        weight = 1.0 / (squares / (m * count) + epsilon)
        columns.append(y.astype(BF16))
        scaled.append(rounded[pl.ds(a, count, stride=rows), :] * weight)
    y = jnp.concatenate(columns, 1)
    hi, lo = halves(jnp.concatenate(scaled, 1))
    across = (((1,), (1,)), ((), ()))
    dots = lax.dot_general(hi, y, across, preferred_element_type=F32) + lax.dot_general(
        lo, y, across, preferred_element_type=F32)
    part[pl.ds(0, count), pl.ds(0, m * count)] = dots / math.sqrt(k_r * k_in)

    def c_copy(k):
        return pltpu.make_async_remote_copy(
            part, parts_in.at[k - 1], c_send.at[k - 1], c_recv.at[k - 1],
            device_id={"hidden": lax.rem(h + k, n)}, device_id_type=MESH)

    for k in range(1, n):
        c_copy(k).start()
    total = part[...]
    for k in range(1, n):
        c_copy(k).wait_recv()
        total = total + parts_in[k - 1]
    cols = score_out.shape[1]
    for place in range(n):
        @pl.when(h == place)
        def _():
            score_out[...] = total[:count, place * cols:(place + 1) * cols]

    @pl.when(h < n - 1)
    def _():
        pltpu.make_async_remote_copy(
            own, pin, p_send.at[0], p_recv.at[0],
            device_id={"hidden": lax.rem(h + 1, n)}, device_id_type=MESH).wait_send()

    @pl.when(h > 0)
    def _():
        pltpu.make_async_remote_copy(
            own, sin, s_send.at[0], s_recv.at[0],
            device_id={"hidden": lax.rem(h + n - 1, n)}, device_id_type=MESH).wait_send()

    for k in range(1, n):
        f_whole(k).wait_send()
        c_copy(k).wait_send()
    for k in range(1, m):
        g_copy(k).wait_send()


def per_device(n, m, activations, cotangent, up_factor_matrix, input_sketch, rank_sketch):
    tokens, depth = activations.shape
    count = tokens // SEQ
    low, k_r = rank_sketch.shape
    k_in = input_sketch.shape[1]
    rows = k_r // n
    used = count * rows
    padded = -(-used // 16) * 16
    lanes = -(-m * count // 128) * 128
    pieces, width = count * PARTS, SEQ // PARTS
    vm, dma = pltpu.VMEM, pltpu.SemaphoreType.DMA
    piece = vm((pieces, k_r, width), F32)
    return pl.pallas_call(
        functools.partial(kernel, n, m),
        out_shape=(
            jax.ShapeDtypeStruct((count, rows * k_in), BF16),
            jax.ShapeDtypeStruct((count, m * count // n), F32),
        ),
        in_specs=[pl.BlockSpec(memory_space=pltpu.HBM)] * 5,
        out_specs=(pl.BlockSpec(memory_space=pltpu.VMEM),) * 2,
        scratch_shapes=[
            vm((count, SEQ, depth), BF16),
            vm((count, SEQ, depth), BF16),
            vm((low, depth), BF16),
            vm((depth, k_in), BF16),
            vm((k_r, low), F32),
            vm((depth, 2 * k_r), BF16),
            vm((count, SEQ, 2 * k_in), BF16),
            piece, piece, piece, piece, piece,
            vm((n, count, rows, k_in), F32),
            vm((n - 1, count, rows, k_in), F32),
            vm((used, k_in), F32),
            vm((padded, k_in), BF16),
            vm((m - 1, padded, k_in), BF16),
            vm((m * used, k_in), F32),
            vm((8, lanes), F32),
            vm((n - 1, 8, lanes), F32),
            dma((2 * count + 3,)),
            dma((1,)), dma((pieces,)), dma((1,)), dma((pieces,)),
            dma((n - 1,)), dma((n - 1,)),
            dma((m - 1,)), dma((m - 1,)),
            dma((n - 1,)), dma((n - 1,)),
        ],
        compiler_params=pltpu.CompilerParams(
            collective_id=0, has_side_effects=True, vmem_limit_bytes=64 * 2**20),
        cost_estimate=pl.CostEstimate(
            flops=2 * tokens * depth * (2 * k_r + k_in),
            bytes_accessed=4 * tokens * depth, transcendentals=0),
    )(activations, cotangent, up_factor_matrix.T, input_sketch, rank_sketch.T)


def solution(mesh):
    placed = (
        P(("groups", "dp"), "hidden"),
        P(("groups", "dp"), "hidden"),
        P("hidden", None),
        P("hidden", None),
        P(),
    )
    return jax.shard_map(
        functools.partial(per_device, mesh.shape["hidden"], mesh.shape["dp"]),
        mesh=mesh,
        in_specs=placed,
        out_specs=(P(("groups", "dp"), "hidden"), P(("groups", "dp"), "hidden")),
        check_vma=False,
    )
```

time: 46.4 us -> 41 us (0.88)
  Pallas kernels: 41.2 us -> 37.4 us
  local copies, waits for them, and re-layouts: 4.26 us -> 2.59 us
    pallas_call x1, Pallas kernels: 41.2 us -> 37.4 us  [per_device(): pl.pallas_call(functools.partial(kernel, n, m), out_shape=(jax.ShapeDtype...]
    unnamed x6 -> x2, local copies, waits for them, and re-layouts: 4.26 us -> 2.59 us
where the time goes in v2:
time: 41 us; the launch traced here: 40.7 us
  Pallas kernels  37.4 us (91%)
  local copies, waits for them, and re-layouts  2.59 us (6%)
  between operations  0.64 us (2%)
    pallas_call x1, Pallas kernels, per_device(): pl.pallas_call(functools.partial(kernel, n, m), out_shape=(jax.ShapeDtype...  37.4 us
    unnamed x2, local copies, waits for them, and re-layouts  2.59 us

profile of v2, /device:TPU:0, one launch (start us, length us, event | category | flops | bytes accessed | tf_op | source)
XLA Modules:
  0.0 40.7 jit_solution(8754918233121794482)
XLA Ops:
  0.6 37.4 %shard_map.68 = (bf16[6,1024]{1,0:T(8,128)(2,1)}, f32[6,6]{1,0:T(8,128)}) custom-call(bf16[3072,2048]{1,0:T(8,128)(2,1)} %act.1, bf16[3072,2048]{1,0:T(8,128)(2,1)} %cot.1, bf16[64,2048]{1,0:T(8,128)(2,1)} %bitcast.2, bf16[2048,128]{1,0:T(8,128)(2,1)} %sketch.1, f32[32,64]{1,0:T(8,128)} %bitcast.3), custom_call_target="tpu_custom_call" | custom-call | flops 2415919104 | bytes 25165824 | tf_op jit(solution)/shard_map/pallas_call | solution.py:298
  38.1 1.3 %copy.9 = bf16[6,1024]{1,0:T(8,128)(2,1)} copy(bf16[6,1024]{1,0:T(8,128)(2,1)} %get-tuple-element.4) | data formatting | bytes 24576
  39.4 1.3 %copy.10 = f32[6,6]{1,0:T(8,128)} copy(f32[6,6]{1,0:T(8,128)} %get-tuple-element.5) | data formatting | bytes 288

commit v3 on v2

--- a/solution.py
+++ b/solution.py
@@ -11,7 +11,7 @@
 SEQ = 512
 PARTS = 2
 AHEAD = 4
-LAG = 3
+LAG = 2
 epsilon = 1e-05
 MESH = pl.DeviceIdType.MESH
 F32, BF16 = jnp.float32, jnp.bfloat16
@@ -92,21 +92,23 @@
             device_id={"hidden": lax.rem(h + n - 1, n)}, device_id_type=MESH)
 
     def forward(step):
-        q = step - LAG * h
-
-        @pl.when((h > 0) & (h < n - 1) & (q >= 0) & (q < pieces))
-        def _():
-            to_right(pout, q).wait_recv()
-            pout[q] = pin[q] + own[q]
-            to_right(pout, q).start()
-
-        p = step - LAG * (n - 1 - h)
-
-        @pl.when((h > 0) & (h < n - 1) & (p >= 0) & (p < pieces))
-        def _():
-            to_left(sout, p).wait_recv()
-            sout[p] = sin[p] + own[p]
-            to_left(sout, p).start()
+        c = step - LAG * h
+
+        @pl.when((h > 0) & (h < n - 1) & (c >= 0) & (c < count))
+        def _():
+            for q in [c * PARTS + j for j in range(PARTS)]:
+                to_right(pout, q).wait_recv()
+                pout[q] = pin[q] + own[q]
+                to_right(pout, q).start()
+
+        e = step - LAG * (n - 1 - h)
+
+        @pl.when((h > 0) & (h < n - 1) & (e >= 0) & (e < count))
+        def _():
+            for q in [e * PARTS + j for j in range(PARTS)]:
+                to_left(sout, q).wait_recv()
+                sout[q] = sin[q] + own[q]
+                to_left(sout, q).start()
 
     def f_copy(k, c):
         return pltpu.make_async_remote_copy(
@@ -153,21 +155,6 @@
 
     lax.fori_loop(0, count, rank_step, 0)
     load_sketch.wait()
-
-    def input_step(c, carry):
-        load_act(c).wait()
-
-        @pl.when(c + AHEAD < count)
-        def _():
-            load_act(c + AHEAD).start()
-
-        side = jnp.dot(actv[c], skv[...], preferred_element_type=F32)
-        hi, lo = halves(side)
-        inp[c] = jnp.concatenate([hi, lo], 1)
-        forward(count + c)
-        return carry
-
-    lax.fori_loop(0, count, input_step, 0)
 
     def finish(c):
         @pl.when(h == n - 1)
@@ -191,18 +178,27 @@
         for k in range(1, n):
             f_copy(k, c).start()
 
-    late = max(0, -(-(LAG * (n - 2) + pieces - 2 * count) // PARTS) - count)
-
-    def last_step(t, carry):
-        for j in range(PARTS):
-            forward(2 * count + PARTS * t + j)
-        if late:
-            pl.when(t >= late)(lambda: finish(t - late))
-        else:
-            finish(t)
+    first = max(count + 1, LAG * (n - 1) + 1)
+
+    def late_step(step, carry):
+        @pl.when(step < 2 * count)
+        def _():
+            c = step - count
+            load_act(c).wait()
+
+            @pl.when(c + AHEAD < count)
+            def _():
+                load_act(c + AHEAD).start()
+
+            side = jnp.dot(actv[c], skv[...], preferred_element_type=F32)
+            hi, lo = halves(side)
+            inp[c] = jnp.concatenate([hi, lo], 1)
+
+        forward(step)
+        pl.when(step >= first)(lambda: finish(step - first))
         return carry
 
-    lax.fori_loop(0, count + late, last_step, 0)
+    lax.fori_loop(count, first + count, late_step, 0)
 
     for k in range(1, n):
         f_whole(k).wait_recv()
@@ -327,7 +323,7 @@
             dma((n - 1,)), dma((n - 1,)),
         ],
         compiler_params=pltpu.CompilerParams(
-            collective_id=0, has_side_effects=True, vmem_limit_bytes=64 * 2**20),
+            collective_id=0, has_side_effects=True, vmem_limit_bytes=64 * 2**20 - 2**17),
         cost_estimate=pl.CostEstimate(
             flops=2 * tokens * depth * (2 * k_r + k_in),
             bytes_accessed=4 * tokens * depth, transcendentals=0),

time: 41 us -> 39.3 us (0.959)
  Pallas kernels: 37.4 us -> 35.7 us
    pallas_call x1, Pallas kernels: 37.4 us -> 35.7 us  [per_device(): pl.pallas_call(functools.partial(kernel, n, m), out_shape=(jax.ShapeDtype...]
where the time goes in v3:
time: 39.3 us; the launch traced here: 39 us
  Pallas kernels  35.7 us (91%)
  local copies, waits for them, and re-layouts  2.59 us (7%)
  between operations  0.64 us (2%)
    pallas_call x1, Pallas kernels, per_device(): pl.pallas_call(functools.partial(kernel, n, m), out_shape=(jax.ShapeDtype...  35.7 us
    unnamed x2, local copies, waits for them, and re-layouts  2.59 us

profile of v3, /device:TPU:0, one launch (start us, length us, event | category | flops | bytes accessed | tf_op | source)
XLA Modules:
  0.0 39.0 jit_solution(5841917443713154813)
XLA Ops:
  0.6 35.7 %shard_map.68 = (bf16[6,1024]{1,0:T(8,128)(2,1)}, f32[6,6]{1,0:T(8,128)}) custom-call(bf16[3072,2048]{1,0:T(8,128)(2,1)} %act.1, bf16[3072,2048]{1,0:T(8,128)(2,1)} %cot.1, bf16[64,2048]{1,0:T(8,128)(2,1)} %bitcast.2, bf16[2048,128]{1,0:T(8,128)(2,1)} %sketch.1, f32[32,64]{1,0:T(8,128)} %bitcast.3), custom_call_target="tpu_custom_call" | custom-call | flops 2415919104 | bytes 25165824 | tf_op jit(solution)/shard_map/pallas_call | solution.py:294
  36.4 1.3 %copy.9 = bf16[6,1024]{1,0:T(8,128)(2,1)} copy(bf16[6,1024]{1,0:T(8,128)(2,1)} %get-tuple-element.4) | data formatting | bytes 24576
  37.7 1.3 %copy.10 = f32[6,6]{1,0:T(8,128)} copy(f32[6,6]{1,0:T(8,128)} %get-tuple-element.5) | data formatting | bytes 288

commit v4 on v3

--- a/solution.py
+++ b/solution.py
@@ -156,7 +156,7 @@
     lax.fori_loop(0, count, rank_step, 0)
     load_sketch.wait()
 
-    def finish(c):
+    def arrived(c):
         @pl.when(h == n - 1)
         def _():
             for j in range(PARTS):
@@ -167,6 +167,7 @@
             for j in range(PARTS):
                 to_left(sout, c * PARTS + j).wait_recv()
 
+    def outer(c):
         total = jnp.concatenate(
             [own[q] + (pin[q] + sin[q]) for q in [c * PARTS + j for j in range(PARTS)]], 1)
         hi, lo = halves(total)
@@ -178,27 +179,48 @@
         for k in range(1, n):
             f_copy(k, c).start()
 
+    def await_act(c):
+        load_act(c).wait()
+
+        @pl.when(c + AHEAD < count)
+        def _():
+            load_act(c + AHEAD).start()
+
+    def input_side(c):
+        side = jnp.dot(actv[c], skv[...], preferred_element_type=F32)
+        hi, lo = halves(side)
+        inp[c] = jnp.concatenate([hi, lo], 1)
+
     first = max(count + 1, LAG * (n - 1) + 1)
 
-    def late_step(step, carry):
-        @pl.when(step < 2 * count)
-        def _():
-            c = step - count
-            load_act(c).wait()
-
-            @pl.when(c + AHEAD < count)
-            def _():
-                load_act(c + AHEAD).start()
-
-            side = jnp.dot(actv[c], skv[...], preferred_element_type=F32)
-            hi, lo = halves(side)
-            inp[c] = jnp.concatenate([hi, lo], 1)
-
+    def act_step(step, carry):
+        await_act(step - count)
+        input_side(step - count)
         forward(step)
-        pl.when(step >= first)(lambda: finish(step - first))
         return carry
 
-    lax.fori_loop(count, first + count, late_step, 0)
+    def both_step(step, carry):
+        await_act(step - count)
+        forward(step - 1)
+        arrived(step - first)
+        input_side(step - count)
+        outer(step - first)
+        return carry
+
+    def outer_step(step, carry):
+        forward(step - 1)
+        arrived(step - first)
+        outer(step - first)
+        return carry
+
+    split = min(first, 2 * count)
+    lax.fori_loop(count, split - 1, act_step, 0)
+    await_act(split - 1 - count)
+    input_side(split - 1 - count)
+    lax.fori_loop(split, 2 * count, both_step, 0)
+    for step in range(2 * count, first):
+        forward(step - 1)
+    lax.fori_loop(max(first, 2 * count), first + count, outer_step, 0)
 
     for k in range(1, n):
         f_whole(k).wait_recv()

time: 39.3 us -> 39.2 us (level)
  no operation moved by 1% of the time
where the time goes in v4:
time: 39.2 us; the launch traced here: 38.8 us
  Pallas kernels  35.6 us (91%)
  local copies, waits for them, and re-layouts  2.59 us (7%)
  between operations  0.64 us (2%)
    pallas_call x1, Pallas kernels, per_device(): pl.pallas_call(functools.partial(kernel, n, m), out_shape=(jax.ShapeDtype...  35.6 us
    unnamed x2, local copies, waits for them, and re-layouts  2.59 us

profile of v4, /device:TPU:0, one launch (start us, length us, event | category | flops | bytes accessed | tf_op | source)
XLA Modules:
  0.0 38.8 jit_solution(7605694978625137511)
XLA Ops:
  0.6 35.6 %shard_map.68 = (bf16[6,1024]{1,0:T(8,128)(2,1)}, f32[6,6]{1,0:T(8,128)}) custom-call(bf16[3072,2048]{1,0:T(8,128)(2,1)} %act.1, bf16[3072,2048]{1,0:T(8,128)(2,1)} %cot.1, bf16[64,2048]{1,0:T(8,128)(2,1)} %bitcast.2, bf16[2048,128]{1,0:T(8,128)(2,1)} %sketch.1, f32[32,64]{1,0:T(8,128)} %bitcast.3), custom_call_target="tpu_custom_call" | custom-call | flops 2415919104 | bytes 25165824 | tf_op jit(solution)/shard_map/pallas_call | solution.py:316
  36.3 1.3 %copy.9 = bf16[6,1024]{1,0:T(8,128)(2,1)} copy(bf16[6,1024]{1,0:T(8,128)(2,1)} %get-tuple-element.4) | data formatting | bytes 24576
  37.6 1.3 %copy.10 = f32[6,6]{1,0:T(8,128)} copy(f32[6,6]{1,0:T(8,128)} %get-tuple-element.5) | data formatting | bytes 288
